TPU v7x, 128 devices: a whole 4x4x4 slice. The times are simulated.
128 devices in a mesh: req: 8 (over y_lo, x), exp: 16 (over z, y_hi, core).
Axes of the slice: x: 4, y: 4 (y_hi: 2, y_lo: 2; y = y_hi * 2 + y_lo), z: 4, core: 2. Of those that a mesh axis runs over, the one named last changes fastest.
Arguments:
- hidden_in: bfloat16 [2048, 6144], P(('req', 'exp')), may hold values from -6 to 6
- queries: bfloat16 [2048, 6144], P('req', 'exp'), may hold values from -25 to 25
- question_kv: bfloat16 [2048, 2048], P('req'), may hold values from -6 to 6
- passage_kv: bfloat16 [32, 2048, 2048], P('req', 'exp'), may hold values from -25 to 25
- use_lists: int32 [8, 4], replicated, may hold values from 0 to 31, as said below
- offsets: int32 [8, 4], replicated, may hold values from 0 to 6399, as said below
- out_weight: bfloat16 [6144, 6144], P('exp', 'req'), may hold values from -0.078125 to 0.078125
- norm_gain: float32 [6144], replicated, may hold values from 0.1 to 1.9
- router: bfloat16 [6144, 8], replicated, may hold values from -0.078125 to 0.078125
- routes: int32 [2048, 2], P(('req', 'exp')), may hold values from 0 to 7, all different within a row; in each aligned block of 16 rows (0 to 15, 16 to 31, ...) at most 5 rows name the same one
- w_gate: bfloat16 [8, 6144, 8192], P('req', None, 'exp'), may hold values from -0.078125 to 0.078125
- w_up: bfloat16 [8, 6144, 8192], P('req', None, 'exp'), may hold values from -0.078125 to 0.078125
- w_down: bfloat16 [8, 8192, 6144], P('req', 'exp'), may hold values from -0.0625 to 0.0625
Outputs:
- layer_out: bfloat16 [2048, 6144], P(('req', 'exp'))
Inputs may be any that keep to these rules, and one draw needn't show every extreme that they name: `use_lists`: passage p lies with owner p // 4; the 4 passages of one request lie with 4 different owners. `offsets`: slot j starts at j * (2112) plus 0 to 63 positions. `routes`: in the rows of one device no expert is named more than 5 times; the two experts of a row differ.
All inputs are finite; a program needn't handle non-finite values.
Results may differ from a plain program's by a relative error of at most 0.014.
Values may be sent and summed in bfloat16 or wider, within the bound.
A program may use at most 128 MiB of HBM per device.

v0:
```python
import math

import jax
import jax.numpy as jnp
import numpy as np
from jax import lax
from jax.experimental import pallas as pl
from jax.experimental.pallas import tpu as pltpu
from jax.sharding import PartitionSpec as P

D = 6144
HALF = D // 2
HQ = 48
KVH = 8
HD = 128
E = 8
PLEN = 2048
PUSE = 4
PASS_DEV = 4
GAP = 64
C = 5
QTOK = 256
TOK = 16
N_REQ = 8
HID = 512
COLS = D // N_REQ
HEADS = 3
ROPE_BASE = 1000000.0
EPSILON = 1e-05
MESH = pl.DeviceIdType.MESH
F32 = jnp.float32
BF16 = jnp.bfloat16
VMEM = pl.BlockSpec(memory_space=pltpu.VMEM)
SMEM = pl.BlockSpec(memory_space=pltpu.SMEM)
ANY = pl.BlockSpec(memory_space=pl.ANY)
SCALE2 = math.log2(math.e) / math.sqrt(HD)
CHUNKS = (0, 1, 3, 2)
LATE = (0,)
NCH = 3
CW = HALF // NCH
CUT = CW // 2


def place():
    req = lax.axis_index("req")
    exp = lax.axis_index("exp")
    return req, exp, exp // 4, (exp // 2) % 2, exp % 2


def member(z, yh, c):
    return (z * 2 + yh) * 2 + c


def remote(src, dst, send, recv, device):
    return pltpu.make_async_remote_copy(
        src_ref=src, dst_ref=dst, send_sem=send, recv_sem=recv, device_id=device, device_id_type=MESH
    )


def greet(devices):
    barrier = pltpu.get_barrier_semaphore()
    for device in devices:
        pl.semaphore_signal(barrier, inc=1, device_id=device, device_id_type=MESH)
    pl.semaphore_wait(barrier, len(devices))


def turn(vectors, cosine, sine):
    return vectors * cosine + pltpu.roll(vectors, HD // 2, vectors.ndim - 1) * sine


def loop(count, body):
    lax.fori_loop(0, count, lambda k, carry: (body(k), carry)[1], 0)


def attention_kernel(
    table, pkv, q_h, qkv, qcos_h, qsin_h, pcos_h, psin_h, w_h, hid_h, gain_h, router_h,
    routes, resid_out, packed_out, gates_out,
    land0, land1, land2, land3, stage, got0, got1, got2, got3,
    kown, ksib, q_in, kvq, qcos, qsin, pcos, psin, qrot, acc, top, low,
    att, w, hid, gain, router, attb, ownp, sibs, sibr, rss, rsr, fsend, fin, nsend, nbuf, pbuf, gbuf,
    ls, s1s, s1r, s2s, s2r, fs, fr,
    a_s, a_r, b_s, b_r, c_s, c_r, d_s, d_r, e_s, e_r,
):
    req, exp, z, yh, c = place()
    x, yl = req % 4, req // 4
    chip = exp // 2
    mine = req * 2 + yh
    land = (land0, land1, land2, land3)
    got = (got0, got1, got2, got3)
    sibling = (req, member(z, yh, 1 - c))
    chips = [(req, ((chip + d) % 8) * 2 + c) for d in range(1, 8)]
    peers = [((req + d) % N_REQ, exp) for d in range(1, 8)]
    beside = ((1 - yl) * 4 + x, exp)
    right, left = (yl * 4 + (x + 1) % 4, exp), (yl * 4 + (x + 3) % 4, exp)

    loads = [
        pltpu.make_async_copy(src, dst, ls.at[i])
        for i, (src, dst) in enumerate(
            (
                (q_h, q_in),
                (qkv.at[:, pl.ds(pl.multiple_of(chip * 256, 256), 256)], kvq),
                (qcos_h, qcos), (qsin_h, qsin), (pcos_h, pcos), (psin_h, psin),
                (w_h, w), (hid_h, hid), (gain_h, gain), (router_h, router),
            )
        )
    ]
    for cp in loads:
        cp.start()

    devices = [(req, member((z + d) % 4, y, c)) for d in range(1, 4) for y in (yh, 1 - yh)]
    devices.append(sibling)
    for k in range(1, 16):
        there = (mine + k) % 16
        devices.append((there // 2, member(z, there % 2, c)))
    greet(devices)

    def cols(zt):
        return pl.ds(pl.multiple_of(zt * 512, 512), 512)

    def first(d):
        zt = (z + d) % 4
        return remote(
            pkv.at[:, :, cols(zt)], land[4 - d], s1s.at[d], s1r.at[4 - d], (req, member(zt, yh, c))
        )

    firsts = {d: first(d) for d in range(1, 4)}
    local = pltpu.make_async_copy(pkv.at[:, :, cols(z)], land0, s1r.at[0])
    local.start()
    firsts[1].start()
    firsts[3].start()

    def half(yt):
        return pl.ds(pl.multiple_of(yt * 256, 256), 256)

    def second(i, k):
        there = (mine + k) % 16
        return remote(
            stage.at[i, there // 2, :, half(there % 2)], got[i].at[mine],
            s2s.at[i, k], s2r.at[i, mine], (there // 2, member(z, there % 2, c)),
        )

    def second_in(i, k):
        there = (mine + k) % 16
        return remote(
            stage.at[i, there // 2, :, half(there % 2)], got[i].at[there],
            s2s.at[i, k], s2r.at[i, there], (there // 2, member(z, there % 2, c)),
        )

    def second_local(i):
        return pltpu.make_async_copy(
            stage.at[i, req, :, half(yh)], got[i].at[mine], s2r.at[i, mine]
        )

    sel = []
    for r in range(N_REQ):
        at = jnp.int32(0)
        for j in range(PUSE):
            p = table[r, j]
            at = at + jnp.where(p // PASS_DEV == req, p % PASS_DEV, 0)
        sel.append(at)
    own = [table[req, j] // PASS_DEV for j in range(PUSE)]
    spot = [
        j * GAP + jnp.clip(table[req, PUSE + j] - j * (PLEN + GAP), 0, GAP - 1) for j in range(PUSE)
    ]

    for i, d in enumerate(CHUNKS):
        if d == 0:
            local.wait()
        else:
            firsts[4 - d].wait_recv()
        for r in range(N_REQ):
            stage[i, r] = land[d][sel[r]]
        loop(15, lambda k: second(i, k + 1).start())
        second_local(i).start()
        if i == 1:
            firsts[2].start()

        if i == 0:
            for cp in loads:
                cp.wait()
            cosine, sine = qcos[...], qsin[...]
            for h in range(HEADS):
                qrot[h * QTOK : (h + 1) * QTOK] = turn(
                    q_in[:, h * HD : (h + 1) * HD].astype(F32), cosine, sine
                ).astype(BF16)
            keys = turn(kvq[:, :HD].astype(F32), cosine, sine).astype(BF16)
            s = lax.dot_general(
                qrot[...], keys, (((1,), (1,)), ((), ())), preferred_element_type=F32
            )
            row = lax.broadcasted_iota(jnp.int32, s.shape, 0) % QTOK
            col = lax.broadcasted_iota(jnp.int32, s.shape, 1)
            s = jnp.where(col <= row, s, -jnp.inf)
            t = jnp.max(s, axis=-1, keepdims=True)
            p = jnp.exp2(s * SCALE2 - t * SCALE2)
            top[...] = jnp.broadcast_to(t, top.shape)
            low[...] = jnp.broadcast_to(jnp.sum(p, axis=-1, keepdims=True), low.shape)
            acc[...] = jnp.dot(p.astype(BF16), kvq[:, HD:], preferred_element_type=F32)

    def attend(block):
        s = lax.dot_general(
            qrot[...], block[:, :HD], (((1,), (1,)), ((), ())), preferred_element_type=F32
        )
        before = top[:, :1]
        t = jnp.maximum(before, jnp.max(s, axis=-1, keepdims=True))
        p = jnp.exp2(s * SCALE2 - t * SCALE2)
        alpha = jnp.exp2((before - t) * SCALE2)
        top[...] = jnp.broadcast_to(t, top.shape)
        low[...] = low[...] * alpha + jnp.sum(p, axis=-1, keepdims=True)
        acc[...] = acc[...] * alpha + jnp.dot(
            p.astype(BF16), block[:, HD:], preferred_element_type=F32
        )

    passes = []
    for i in range(4):
        loop(15, lambda k: second_in(i, k + 1).wait_recv())
        second_local(i).wait()
        for j in range(PUSE):
            cosine, sine = pcos[pl.ds(spot[j], 1), :], psin[pl.ds(spot[j], 1), :]
            for y in range(2):
                kv = got[i][own[j] * 2 + y]
                rows = pl.ds(j * 256 + y * 128, 128)
                kown[i, rows, :HD] = turn(kv[:, :HD].astype(F32), cosine, sine).astype(BF16)
                kown[i, rows, HD:] = kv[:, HD:]
        cp = remote(kown.at[i], ksib.at[i], fs.at[i], fr.at[i], sibling)
        cp.start()
        passes.append(cp)
        attend(kown.at[i])
        cp.wait_recv()
        attend(ksib.at[i])

    for h in range(HEADS):
        rows = pl.ds(h * QTOK, QTOK)
        att[:, :, :, h * HD : (h + 1) * HD] = (
            (acc[rows, :] / low[rows, :]).astype(BF16).reshape(8, 2, TOK, HD)
        )

    def gather(i, src, xr, side, device):
        cp = remote(src, attb.at[xr, side], a_s.at[i], a_r.at[i], device)
        cp.start()
        return cp

    swap = gather(0, att, 0, 1, beside)
    right0 = gather(1, att, 3, 0, right)
    left0 = gather(2, att, 1, 0, left)

    def multiply(k, source):
        theirs = source[:, 1 - c].reshape(128, 384)
        sibs[k] = jnp.dot(theirs, w[...], preferred_element_type=F32).astype(BF16).reshape(8, TOK, COLS)
        cp = remote(sibs.at[k], sibr.at[k], b_s.at[k], b_r.at[k], sibling)
        cp.start()
        ours = source[:, c].reshape(128, 384)
        ownp[k] = jnp.dot(ours, w[...], preferred_element_type=F32).reshape(8, TOK, COLS)
        return cp

    def scatter(k, cp):
        cp.wait_recv()
        rss[k] = (ownp[k] + sibr[k].astype(F32)).astype(BF16)
        rsr[k, chip] = rss[k, chip]
        copies = []
        for d in range(1, 8):
            there = (chip + d) % 8
            cp = remote(rss.at[k, there], rsr.at[k, chip], c_s.at[k, d], c_r.at[k, d], chips[d - 1])
            cp.start()
            copies.append(cp)
        return copies

    order = ((0, 0), (0, 1), (3, 0), (1, 0), (1, 1), (3, 1), (2, 0), (2, 1))

    def finish(k, copies):
        for cp in copies:
            cp.wait_recv()
        total = jnp.sum(rsr[k].astype(F32), axis=0).astype(BF16)
        if k == 0:
            fin[req] = total
            return None
        fsend[k] = total
        xr, side = order[k]
        target = (jnp.abs(yl - side) * 4 + (x + xr) % 4, exp)
        cp = remote(fsend.at[k], fin.at[req], d_s.at[k], d_r.at[k], target)
        cp.start()
        return cp

    halves, parts, ends, gathers = {}, {}, {}, [swap, right0, left0]
    for k in range(8 + 4):
        if k < 8:
            if k == 1:
                swap.wait_recv()
                right1 = gather(3, attb.at[0, 1], 3, 1, right)
                left1 = gather(4, attb.at[0, 1], 1, 1, left)
                right0.wait_recv()
                right2 = gather(5, attb.at[3, 0], 2, 0, right)
                gathers += [right1, left1, right2]
            elif k == 3:
                left0.wait_recv()
            elif k == 4:
                left1.wait_recv()
                left2 = gather(6, attb.at[1, 1], 2, 1, left)
                gathers.append(left2)
            elif k == 5:
                right1.wait_recv()
            elif k == 6:
                right2.wait_recv()
            elif k == 7:
                left2.wait_recv()
            halves[k] = multiply(k, att if k == 0 else attb.at[order[k][0], order[k][1]])
        if 0 <= k - 1 < 8:
            parts[k - 1] = scatter(k - 1, halves[k - 1])
        if 0 <= k - 4 < 8:
            ends[k - 4] = finish(k - 4, parts[k - 4])
    for k in range(1, 8):
        ends[k].wait_recv()

    attn = jnp.concatenate([fin[i] for i in range(N_REQ)], axis=1).astype(F32)
    resid = hid[...].astype(F32) + attn
    resid_out[...] = resid
    mean = jnp.mean(resid * resid, axis=-1, keepdims=True)
    normed = (resid * lax.rsqrt(mean + EPSILON) * gain[...]).astype(BF16)
    left_half, right_half = normed[:, :HALF], normed[:, HALF:]
    nsend[...] = jnp.where(c == 0, right_half, left_half)
    nbuf[c] = jnp.where(c == 0, left_half, right_half)
    lasts = [remote(nsend, nbuf.at[c], e_s.at[0], e_r.at[0], sibling)]
    lasts[0].start()

    row = lax.broadcasted_iota(jnp.int32, (TOK, TOK), 0)
    col = lax.broadcasted_iota(jnp.int32, (TOK, TOK), 1)
    named = lax.broadcasted_iota(jnp.int32, (TOK, E), 1)
    places = lax.broadcasted_iota(jnp.int32, (TOK, 128), 1)
    choice, hits = [], []
    for k in range(2):
        expert = jnp.sum(jnp.where(row == col, routes[k : k + 1, :], 0), axis=1, keepdims=True)
        choice.append(expert)
        hits.append((named == expert).astype(F32))
    earlier = jnp.dot(
        (col < row).astype(BF16), (hits[0] + hits[1]).astype(BF16), preferred_element_type=F32
    )
    matches = []
    for k in range(2):
        rank = jnp.sum(hits[k] * earlier, axis=1, keepdims=True).astype(jnp.int32)
        matches.append((places == choice[k] * TOK + c * C + rank).astype(F32))
    pbuf[c] = (matches[0] + matches[1]).astype(BF16)
    logits = lax.dot_general(
        normed, router[...], (((1,), (1,)), ((), ())), preferred_element_type=F32
    )
    apart = jnp.sum(logits * (hits[0] - hits[1]), axis=-1, keepdims=True)
    gates = matches[0] * jax.nn.sigmoid(apart) + matches[1] * jax.nn.sigmoid(-apart)
    coarse = gates.astype(BF16)
    gbuf[c, 0] = coarse
    gbuf[c, 1] = (gates - coarse.astype(F32)).astype(BF16)
    for i, ref in ((1, pbuf), (2, gbuf)):
        cp = remote(ref.at[c], ref.at[c], e_s.at[i], e_r.at[i], sibling)
        cp.start()
        lasts.append(cp)
    lasts[0].wait_recv()
    lasts[1].wait_recv()
    packed_out[...] = (
        lax.dot_general(
            pbuf[...].reshape(32, 128), nbuf[...].reshape(32, HALF), (((0,), (0,)), ((), ())),
            preferred_element_type=F32,
        )
        .astype(BF16)
        .reshape(E, TOK, HALF)
    )
    lasts[2].wait_recv()
    gates_out[...] = gbuf[...]

    for cp in list(firsts.values()) + passes + gathers + lasts:
        cp.wait_send()
    for i in range(4):
        loop(15, lambda k: second(i, k + 1).wait_send())
    for k in range(8):
        halves[k].wait_send()
        for cp in parts[k]:
            cp.wait_send()
        if k > 0:
            ends[k].wait_send()


def attention(*operands):
    dma = pltpu.SemaphoreType.DMA
    v = pltpu.VMEM
    return pl.pallas_call(
        attention_kernel,
        out_shape=(
            jax.ShapeDtypeStruct((TOK, D), F32),
            jax.ShapeDtypeStruct((E, TOK, HALF), BF16),
            jax.ShapeDtypeStruct((2, 2, TOK, 128), BF16),
        ),
        in_specs=[SMEM] + [ANY] * 11 + [VMEM],
        out_specs=(VMEM,) * 3,
        scratch_shapes=[v((PASS_DEV, 128, 512), BF16)] * 4
        + [v((4, N_REQ, 128, 512), BF16)]
        + [v((16, 128, 256), BF16)] * 4
        + [
            v((4, 1024, 256), BF16), v((4, 1024, 256), BF16),
            v((QTOK, HEADS * HD), BF16), v((QTOK, 256), BF16),
            v((QTOK, HD), F32), v((QTOK, HD), F32),
            v((PUSE * GAP, HD), F32), v((PUSE * GAP, HD), F32),
            v((HEADS * QTOK, HD), BF16),
            v((HEADS * QTOK, HD), F32), v((HEADS * QTOK, HD), F32), v((HEADS * QTOK, HD), F32),
            v((8, 2, TOK, 384), BF16), v((384, COLS), BF16), v((TOK, D), BF16), v((1, D), F32),
            v((E, D), BF16), v((4, 2, 8, 2, TOK, 384), BF16),
            v((8, 8, TOK, COLS), F32),
            v((8, 8, TOK, COLS), BF16), v((8, 8, TOK, COLS), BF16),
            v((8, 8, TOK, COLS), BF16), v((8, 8, TOK, COLS), BF16),
            v((8, TOK, COLS), BF16), v((8, TOK, COLS), BF16),
            v((TOK, HALF), BF16), v((2, TOK, HALF), BF16),
            v((2, TOK, 128), BF16), v((2, 2, TOK, 128), BF16),
            dma((10,)), dma((4,)), dma((4,)), dma((4, 16)), dma((4, 16)), dma((4,)), dma((4,)),
            dma((7,)), dma((7,)), dma((8,)), dma((8,)), dma((8, 8)), dma((8, 8)),
            dma((8,)), dma((8,)), dma((3,)), dma((3,)),
        ],
        name="attend_and_project",
        compiler_params=pltpu.CompilerParams(
            collective_id=0, has_side_effects=True, vmem_limit_bytes=56 << 20
        ),
    )(*operands)


def expert_kernel(
    packed, gates, resid, wg_h, wu_h, wd_h, out,
    wg, wu, wd, prx, xo, xs, gu, inner, po, sps, spr, rzs, rz, ysend, ry, kept, bsend, ret,
    mixed, mrecv,
    w_s, a_s, a_r, y_s, y_r, g_s, g_r, f_s, f_r, p_s, p_r, r_s, r_r, t_s, t_r, m_s, m_r,
):
    req, exp, z, yh, c = place()
    other = 1 - yh
    sibling = (req, member(z, yh, 1 - c))
    across = (req, member(z, other, c))
    up = (req, member((z + 1) % 4, yh, c))
    down = (req, member((z + 3) % 4, yh, c))
    peers = [((req + d) % N_REQ, exp) for d in range(1, 8)]
    loads = [
        pltpu.make_async_copy(src, dst, w_s.at[i])
        for i, (src, dst) in enumerate(((wg_h, wg), (wu_h, wu), (wd_h, wd)))
    ]
    for cp in loads:
        cp.start()
    greet(peers + [sibling, across, up, down])

    started = []

    def go(cp):
        cp.start()
        started.append(cp)
        return cp

    def part(i):
        return pl.ds(i * CW, CW)

    row = lax.broadcasted_iota(jnp.int32, (80, 128), 0)
    col = lax.broadcasted_iota(jnp.int32, (80, 128), 1)
    pick = (col == row // 10 * TOK + row % 10).astype(BF16)
    row = lax.broadcasted_iota(jnp.int32, (128, 80), 1)
    col = lax.broadcasted_iota(jnp.int32, (128, 80), 0)
    spread = (col == row // 10 * TOK + row % 10).astype(BF16)

    arrive = []
    for i in range(NCH):
        copies = []
        for d in range(1, 8):
            there = (req + d) % N_REQ
            copies.append(
                go(remote(
                    packed.at[there, :, part(i)], prx.at[i, req], a_s.at[i, d], a_r.at[i, d], peers[d - 1]
                ))
            )
        prx[i, req] = packed[req, :, i * CW : (i + 1) * CW]
        arrive.append(copies)

    def ring(n, i, src_at, dst_at, device):
        return go(remote(
            xo.at[(i,) + src_at], xo.at[(i,) + dst_at], g_s.at[n, i], g_r.at[n, i], device
        ))

    shares = {}

    def share(i, zr, y, second):
        at = zr * 2 + second
        shares[i, zr, second] = go(remote(
            xo.at[i, zr, y], xs.at[i, zr, y], f_s.at[at, i], f_r.at[at, i], sibling
        ))

    swap, up1, down1, up2, down2, up3, down3 = {}, {}, {}, {}, {}, {}, {}
    over1, over2, over3 = {}, {}, {}
    lower, upper = (slice(None), pl.ds(0, CUT)), (slice(None), pl.ds(CUT, CUT))
    for i in range(NCH):
        for cp in arrive[i]:
            cp.wait_recv()
        xo[i, 0, yh] = jnp.dot(
            pick, prx[i].reshape(128, CW), preferred_element_type=F32
        ).astype(BF16)
        swap[i] = ring(0, i, (0, yh), (0, yh), across)
        up1[i] = ring(1, i, (0, yh), (3, yh), up)
        down1[i] = ring(2, i, (0, yh), (1, yh), down)
        share(i, 0, yh, 0)
    for i in range(NCH):
        if i in LATE:
            up1[i].wait_recv()
            up3[i] = ring(5, i, (3, yh) + lower, (2, yh) + lower, up)
            over3[i] = ring(3, i, (3, yh), (3, yh), across)
            share(i, 3, yh, 0)
            down1[i].wait_recv()
            down3[i] = ring(6, i, (1, yh) + upper, (2, yh) + upper, down)
            over1[i] = ring(4, i, (1, yh), (1, yh), across)
            share(i, 1, yh, 0)
            swap[i].wait_recv()
            share(i, 0, other, 1)
        else:
            swap[i].wait_recv()
            up2[i] = ring(3, i, (0, other), (3, other), up)
            down2[i] = ring(4, i, (0, other), (1, other), down)
            share(i, 0, other, 1)
            up1[i].wait_recv()
            up3[i] = ring(5, i, (3, yh), (2, yh), up)
            share(i, 3, yh, 0)
            down1[i].wait_recv()
            share(i, 1, yh, 0)

    def hidden(i, zr):
        shares[i, zr, 0].wait_recv()
        shares[i, zr, 1].wait_recv()
        near = pl.ds(pl.multiple_of(c * HALF + i * CW, CW), CW)
        far = pl.ds(pl.multiple_of((1 - c) * HALF + i * CW, CW), CW)
        a, b = xo[i, zr].reshape(160, CW), xs[i, zr].reshape(160, CW)
        for n, weights in enumerate((wg, wu)):
            value = jnp.dot(a, weights[near, :], preferred_element_type=F32)
            value = value + jnp.dot(b, weights[far, :], preferred_element_type=F32)
            if i > 0:
                value = value + gu[zr, n]
            gu[zr, n] = value

    sums = {}

    def result(zr):
        inner[...] = (jax.nn.silu(gu[zr, 0]) * gu[zr, 1]).astype(BF16)
        for i in range(NCH):
            near = pl.ds(pl.multiple_of(c * HALF + i * CW, CW), CW)
            far = pl.ds(pl.multiple_of((1 - c) * HALF + i * CW, CW), CW)
            sps[i, zr] = (
                jnp.dot(inner[...], wd[:, far], preferred_element_type=F32)
                .astype(BF16)
                .reshape(2, 80, CW)
            )
            sums[i, zr] = go(remote(
                sps.at[i, zr], spr.at[i, zr], p_s.at[i, zr], p_r.at[i, zr], sibling
            ))
            po[i, zr] = (
                jnp.dot(inner[...], wd[:, near], preferred_element_type=F32)
                .astype(BF16)
                .reshape(2, 80, CW)
            )

    def total(i, zr, y):
        return po[i, zr, y].astype(F32) + spr[i, zr, y].astype(F32)

    def pass_on(n, i, value, device):
        rzs[n, i] = value.astype(BF16)
        return go(remote(rzs.at[n, i], rz.at[n, i], r_s.at[n, i], r_r.at[n, i], device))

    loads[0].wait()
    loads[1].wait()
    for i in range(NCH):
        hidden(i, 0)
    for i in range(NCH):
        if i in LATE:
            up3[i].wait_recv()
            down3[i].wait_recv()
            over2[i] = ring(7, i, (2, yh), (2, yh), across)
            share(i, 2, yh, 0)
            over1[i].wait_recv()
            share(i, 1, other, 1)
            over3[i].wait_recv()
            share(i, 3, other, 1)
        else:
            down2[i].wait_recv()
            down3[i] = ring(6, i, (1, other), (2, other), down)
            share(i, 1, other, 1)
            up2[i].wait_recv()
            share(i, 3, other, 1)
        hidden(i, 1)
        hidden(i, 3)
    loads[2].wait()
    result(1)
    result(3)
    early = [i for i in range(NCH) if i not in LATE]
    to_up, to_down, far_up, far_down, near_up, near_down = {}, {}, {}, {}, {}, {}
    cross, cross1, cross2, cross3, back = {}, {}, {}, {}, {}
    for i in range(NCH):
        sums[i, 1].wait_recv()
        sums[i, 3].wait_recv()
        if i in LATE:
            cross1[i] = pass_on(0, i, total(i, 1, other), across)
            cross3[i] = pass_on(1, i, total(i, 3, other), across)
        else:
            to_up[i] = pass_on(0, i, total(i, 1, other), up)
            to_down[i] = pass_on(1, i, total(i, 3, yh), down)
    for i in range(NCH):
        if i in LATE:
            over2[i].wait_recv()
            share(i, 2, other, 1)
        else:
            up3[i].wait_recv()
            share(i, 2, yh, 0)
            down3[i].wait_recv()
            share(i, 2, other, 1)
        if i > 0:
            hidden(i - 1, 2)
    hidden(NCH - 1, 2)
    result(2)
    for i in range(NCH):
        sums[i, 2].wait_recv()
        if i in LATE:
            cross2[i] = pass_on(6, i, total(i, 2, other), across)
        else:
            far_up[i] = pass_on(2, i, total(i, 2, yh), up)
            far_down[i] = pass_on(3, i, total(i, 2, other), down)
    result(0)

    def cross_over(i, value):
        ysend[i] = value.astype(BF16)
        cross[i] = go(remote(ysend.at[i], ry.at[i], y_s.at[i], y_r.at[i], across))

    for i in LATE:
        sums[i, 0].wait_recv()
        cross_over(i, total(i, 0, other))
        cross2[i].wait_recv()
        both = (total(i, 2, yh) + rz[6, i].astype(F32)).astype(BF16)
        rzs[2, i, :, :CUT] = both[:, :CUT]
        rzs[3, i, :, CUT:] = both[:, CUT:]
        for n, cols, device, copies in ((2, lower, up, far_up), (3, upper, down, far_down)):
            copies[i] = go(remote(
                rzs.at[(n, i) + cols], rz.at[(n, i) + cols], r_s.at[n, i], r_r.at[n, i], device
            ))
    for i in early:
        far_up[i].wait_recv()
        near_up[i] = pass_on(4, i, total(i, 1, yh) + rz[2, i].astype(F32), up)
        far_down[i].wait_recv()
        near_down[i] = pass_on(5, i, total(i, 3, other) + rz[3, i].astype(F32), down)
    for i in LATE:
        cross1[i].wait_recv()
        cross3[i].wait_recv()
        far_up[i].wait_recv()
        far_down[i].wait_recv()
        ahead = total(i, 1, yh) + rz[0, i].astype(F32)
        behind = total(i, 3, yh) + rz[1, i].astype(F32)
        added = jnp.concatenate(
            [ahead[:, :CUT] + rz[2, i, :, :CUT].astype(F32), ahead[:, CUT:]], axis=1
        )
        near_up[i] = pass_on(4, i, added, up)
        added = jnp.concatenate(
            [behind[:, :CUT], behind[:, CUT:] + rz[3, i, :, CUT:].astype(F32)], axis=1
        )
        near_down[i] = pass_on(5, i, added, down)

    def gathered(i):
        sums[i, 0].wait_recv()
        to_up[i].wait_recv()
        near_down[i].wait_recv()
        cross_over(i, total(i, 0, other) + rz[0, i].astype(F32) + rz[5, i].astype(F32))
        to_down[i].wait_recv()
        near_up[i].wait_recv()
        kept[i] = total(i, 0, yh) + rz[1, i].astype(F32) + rz[4, i].astype(F32)

    def give_back(i):
        cross[i].wait_recv()
        done = kept[i] + ry[i].astype(F32)
        if i in LATE:
            near_up[i].wait_recv()
            near_down[i].wait_recv()
            done = done + rz[4, i].astype(F32) + rz[5, i].astype(F32)
        bsend[i] = (
            jnp.dot(spread, done.astype(BF16), preferred_element_type=F32)
            .astype(BF16)
            .reshape(N_REQ, TOK, CW)
        )
        copies = []
        for d in range(1, 8):
            there = (req + d) % N_REQ
            copies.append(go(remote(
                bsend.at[i, there], ret.at[i, req], t_s.at[i, d], t_r.at[i, d], peers[d - 1]
            )))
        ret[i, req] = bsend[i, req]
        back[i] = copies

    for i in LATE:
        kept[i] = total(i, 0, yh)
    gathered(early[0])
    for n in range(1, len(early)):
        gathered(early[n])
        give_back(early[n - 1])
    give_back(early[-1])
    for i in LATE:
        give_back(i)
    mix = {}
    for i in early + list(LATE):
        for cp in back[i]:
            cp.wait_recv()
        terms = jnp.dot(
            gates[...].reshape(4 * TOK, 128), ret[i].reshape(128, CW), preferred_element_type=F32
        ).reshape(2, 2, TOK, CW)
        mixed[i] = terms[:, 0] + terms[:, 1]
        mix[i] = go(remote(mixed.at[i, 1 - c], mrecv.at[i], m_s.at[i], m_r.at[i], sibling))
        near = pl.ds(pl.multiple_of(c * HALF + i * CW, CW), CW)
        out[:, near] = (resid[:, near] + mixed[i, c]).astype(BF16)
    for i in early + list(LATE):
        mix[i].wait_recv()
        far = pl.ds(pl.multiple_of((1 - c) * HALF + i * CW, CW), CW)
        out[:, far] = (resid[:, far] + mrecv[i]).astype(BF16)
    for cp in started:
        cp.wait_send()


def experts(*operands):
    dma = pltpu.SemaphoreType.DMA
    v = pltpu.VMEM
    return pl.pallas_call(
        expert_kernel,
        out_shape=jax.ShapeDtypeStruct((TOK, D), BF16),
        in_specs=[VMEM] * 3 + [ANY] * 3,
        out_specs=VMEM,
        scratch_shapes=[
            v((D, HID), BF16), v((D, HID), BF16), v((HID, D), BF16),
            v((NCH, N_REQ, TOK, CW), BF16),
            v((NCH, 4, 2, 80, CW), BF16), v((NCH, 4, 2, 80, CW), BF16),
            v((4, 2, 160, HID), F32),
            v((160, HID), BF16),
            v((NCH, 4, 2, 80, CW), BF16), v((NCH, 4, 2, 80, CW), BF16), v((NCH, 4, 2, 80, CW), BF16),
            v((7, NCH, 80, CW), BF16), v((7, NCH, 80, CW), BF16),
            v((NCH, 80, CW), BF16), v((NCH, 80, CW), BF16), v((NCH, 80, CW), F32),
            v((NCH, N_REQ, TOK, CW), BF16), v((NCH, N_REQ, TOK, CW), BF16),
            v((NCH, 2, TOK, CW), F32), v((NCH, TOK, CW), F32),
            dma((3,)), dma((NCH, 8)), dma((NCH, 8)), dma((NCH,)), dma((NCH,)),
            dma((8, NCH)), dma((8, NCH)), dma((8, NCH)), dma((8, NCH)),
            dma((NCH, 4)), dma((NCH, 4)), dma((7, NCH)), dma((7, NCH)),
            dma((NCH, 8)), dma((NCH, 8)), dma((NCH,)), dma((NCH,)),
        ],
        name="apply_experts",
        compiler_params=pltpu.CompilerParams(
            collective_id=1, has_side_effects=True, vmem_limit_bytes=60 << 20
        ),
    )(*operands)


def rotation(positions):
    steps = np.arange(HD // 2, dtype=np.float32) / np.float32(HD // 2)
    freq = (np.float64(ROPE_BASE) ** -steps.astype(np.float64)).astype(np.float32)
    angles = positions.astype(np.float32)[:, None] * freq[None, :]
    cosine, sine = np.cos(angles.astype(np.float64)), np.sin(angles.astype(np.float64))
    return (
        jnp.asarray(np.concatenate([cosine, cosine], axis=1), F32),
        jnp.asarray(np.concatenate([-sine, sine], axis=1), F32),
    )


def per_device(
    hidden_in, queries, question_kv, passage_kv, use_lists, offsets, out_weight, norm_gain,
    router, routes, w_gate, w_up, w_down,
):
    qcos, qsin = rotation(PUSE * (PLEN + GAP) + np.arange(QTOK))
    starts = np.arange(PUSE)[:, None] * (PLEN + GAP) + np.arange(GAP)[None, :]
    pcos, psin = rotation(starts.reshape(-1))
    resid, packed, gates = attention(
        jnp.concatenate([use_lists, offsets], axis=1), passage_kv, queries, question_kv, qcos, qsin, pcos, psin, out_weight,
        hidden_in, norm_gain.reshape(1, D), router.T, routes.T,
    )
    return experts(packed, gates, resid, w_gate[0], w_up[0], w_down[0])


def solution(mesh):
    in_specs = (
        P(("req", "exp"), None),
        P("req", "exp"),
        P("req", None),
        P("req", "exp", None),
        P(),
        P(),
        P("exp", "req"),
        P(),
        P(),
        P(("req", "exp"), None),
        P("req", None, "exp"),
        P("req", None, "exp"),
        P("req", "exp", None),
    )
    return jax.shard_map(
        per_device, mesh=mesh, in_specs=in_specs, out_specs=P(("req", "exp"), None), check_vma=False
    )
```

profile of v0, /device:TPU:1, one launch (start us, length us, event | category | flops | bytes accessed | tf_op | source)
XLA Modules:
  0.0 196.2 jit_solution(3160240889517169931)
XLA Ops:
  0.0 0.8 copy.18
  0.8 0.8 copy.19
  1.5 0.7 pad_add_fusion.table
  2.2 102.0 %attend_and_project.1 = (f32[16,6144]{1,0:T(8,128)}, bf16[8,16,3072]{2,1,0:T(8,128)(2,1)}, bf16[2,2,16,128]{3,2,1,0:T(8,128)(2,1)}) custom-call(s32[8,8]{1,0:T(8,128)} %pad_add_fusion.table, bf16[4,128,2048]{2,1,0:T(8,128)(2,1)} %pkv.1, bf16[256,384]{1,0:T(8,128)(2,1)} %q_h.1, bf16[256,2048]{1,0:T(8,128)(2,1)} %qkv.1, f32[256,128]{1,0:T(8,128)} %constant.8.clone.qcos_h, ...), custom_call_target="tpu_custom_call" | custom-call | tf_op jit(solution)/shard_map/attend_and_project/pallas_call | solution.py:381
  104.2 90.3 %apply_experts.1 = bf16[16,6144]{1,0:T(8,128)(2,1)} custom-call(bf16[8,16,3072]{2,1,0:T(8,128)(2,1)} %get-tuple-element.8.packed, bf16[2,2,16,128]{3,2,1,0:T(8,128)(2,1)} %get-tuple-element.9.gates, f32[16,6144]{1,0:T(8,128)} %get-tuple-element.10.resid, bf16[6144,512]{1,0:T(8,128)(2,1)} %bitcast.6, bf16[6144,512]{1,0:T(8,128)(2,1)} %bitcast.7, ...), custom_call_target="tpu_custom_call" | custom-call | tf_op jit(solution)/shard_map/apply_experts/pallas_call | solution.py:716
  194.6 1.6 copy.21
where the time goes:
time: 196 us
  Pallas kernels  192 us (98%)
  local copies, waits for them, and re-layouts  3.13 us (2%)
    pallas_call x1, Pallas kernels, attention(): pl.pallas_call(attention_kernel, out_shape=(jax.ShapeDtypeStruct((TOK, D)...  102 us
    pallas_call x1, Pallas kernels, experts(): pl.pallas_call(expert_kernel, out_shape=jax.ShapeDtypeStruct((TOK, D), BF...  90.3 us

commit v1 on v0

--- a/solution.py
+++ b/solution.py
@@ -57,11 +57,15 @@
     )
 
 
-def greet(devices):
+def call_out(devices):
     barrier = pltpu.get_barrier_semaphore()
     for device in devices:
         pl.semaphore_signal(barrier, inc=1, device_id=device, device_id_type=MESH)
-    pl.semaphore_wait(barrier, len(devices))
+
+
+def greet(devices):
+    call_out(devices)
+    pl.semaphore_wait(pltpu.get_barrier_semaphore(), len(devices))
 
 
 def turn(vectors, cosine, sine):
@@ -73,13 +77,12 @@
 
 
 def attention_kernel(
-    table, pkv, q_h, qkv, qcos_h, qsin_h, pcos_h, psin_h, w_h, hid_h, gain_h, router_h,
-    routes, resid_out, packed_out, gates_out,
+    table, pkv, q_h, qkv, qcos_h, qsin_h, pcos_h, psin_h, w_h, attn_out,
     land0, land1, land2, land3, stage, got0, got1, got2, got3,
     kown, ksib, q_in, kvq, qcos, qsin, pcos, psin, qrot, acc, top, low,
-    att, w, hid, gain, router, attb, ownp, sibs, sibr, rss, rsr, fsend, fin, nsend, nbuf, pbuf, gbuf,
+    att, w, attb, ownp, sibs, sibr, rss, rsr, fsend, fin,
     ls, s1s, s1r, s2s, s2r, fs, fr,
-    a_s, a_r, b_s, b_r, c_s, c_r, d_s, d_r, e_s, e_r,
+    a_s, a_r, b_s, b_r, c_s, c_r, d_s, d_r,
 ):
     req, exp, z, yh, c = place()
     x, yl = req % 4, req // 4
@@ -100,7 +103,7 @@
                 (q_h, q_in),
                 (qkv.at[:, pl.ds(pl.multiple_of(chip * 256, 256), 256)], kvq),
                 (qcos_h, qcos), (qsin_h, qsin), (pcos_h, pcos), (psin_h, psin),
-                (w_h, w), (hid_h, hid), (gain_h, gain), (router_h, router),
+                (w_h, w),
             )
         )
     ]
@@ -310,16 +313,89 @@
     for k in range(1, 8):
         ends[k].wait_recv()
 
-    attn = jnp.concatenate([fin[i] for i in range(N_REQ)], axis=1).astype(F32)
-    resid = hid[...].astype(F32) + attn
-    resid_out[...] = resid
-    mean = jnp.mean(resid * resid, axis=-1, keepdims=True)
-    normed = (resid * lax.rsqrt(mean + EPSILON) * gain[...]).astype(BF16)
+    for i in range(N_REQ):
+        attn_out[:, i * COLS : (i + 1) * COLS] = fin[i]
+
+    for cp in list(firsts.values()) + passes + gathers:
+        cp.wait_send()
+    for i in range(4):
+        loop(15, lambda k: second(i, k + 1).wait_send())
+    for k in range(8):
+        halves[k].wait_send()
+        for cp in parts[k]:
+            cp.wait_send()
+        if k > 0:
+            ends[k].wait_send()
+
+
+def attention(*operands):
+    dma = pltpu.SemaphoreType.DMA
+    v = pltpu.VMEM
+    return pl.pallas_call(
+        attention_kernel,
+        out_shape=jax.ShapeDtypeStruct((TOK, D), BF16),
+        in_specs=[SMEM] + [ANY] * 8,
+        out_specs=VMEM,
+        scratch_shapes=[v((PASS_DEV, 128, 512), BF16)] * 4
+        + [v((4, N_REQ, 128, 512), BF16)]
+        + [v((16, 128, 256), BF16)] * 4
+        + [
+            v((4, 1024, 256), BF16), v((4, 1024, 256), BF16),
+            v((QTOK, HEADS * HD), BF16), v((QTOK, 256), BF16),
+            v((QTOK, HD), F32), v((QTOK, HD), F32),
+            v((PUSE * GAP, HD), F32), v((PUSE * GAP, HD), F32),
+            v((HEADS * QTOK, HD), BF16),
+            v((HEADS * QTOK, HD), F32), v((HEADS * QTOK, HD), F32), v((HEADS * QTOK, HD), F32),
+            v((8, 2, TOK, 384), BF16), v((384, COLS), BF16), v((4, 2, 8, 2, TOK, 384), BF16),
+            v((8, 8, TOK, COLS), F32),
+            v((8, 8, TOK, COLS), BF16), v((8, 8, TOK, COLS), BF16),
+            v((8, 8, TOK, COLS), BF16), v((8, 8, TOK, COLS), BF16),
+            v((8, TOK, COLS), BF16), v((8, TOK, COLS), BF16),
+            dma((7,)), dma((4,)), dma((4,)), dma((4, 16)), dma((4, 16)), dma((4,)), dma((4,)),
+            dma((7,)), dma((7,)), dma((8,)), dma((8,)), dma((8, 8)), dma((8, 8)),
+            dma((8,)), dma((8,)),
+        ],
+        name="attend_and_project",
+        compiler_params=pltpu.CompilerParams(
+            collective_id=0, has_side_effects=True, vmem_limit_bytes=56 << 20
+        ),
+    )(*operands)
+
+
+def expert_kernel(
+    attn, routes, hid_h, gain_h, router_h, wg_h, wu_h, wd_h, out,
+    hid, gain, router, resid, packed, nsend, nbuf, pbuf, gates,
+    wg, wu, wd, prx, xo, xs, gu, inner, po, sps, spr, rzs, rz, ysend, ry, kept, bsend, ret,
+    mixed, mrecv,
+    w_s, e_s, e_r, a_s, a_r, y_s, y_r, g_s, g_r, f_s, f_r, p_s, p_r, r_s, r_r, t_s, t_r, m_s, m_r,
+):
+    req, exp, z, yh, c = place()
+    other = 1 - yh
+    sibling = (req, member(z, yh, 1 - c))
+    across = (req, member(z, other, c))
+    up = (req, member((z + 1) % 4, yh, c))
+    down = (req, member((z + 3) % 4, yh, c))
+    peers = [((req + d) % N_REQ, exp) for d in range(1, 8)]
+    loads = [
+        pltpu.make_async_copy(src, dst, w_s.at[i])
+        for i, (src, dst) in enumerate(
+            ((wg_h, wg), (wu_h, wu), (wd_h, wd), (hid_h, hid), (gain_h, gain), (router_h, router))
+        )
+    ]
+    for cp in loads[3:] + loads[:3]:
+        cp.start()
+    friends = peers + [sibling, across, up, down]
+    call_out(friends)
+
+    for cp in loads[3:]:
+        cp.wait()
+    stream = hid[...].astype(F32) + attn[...].astype(F32)
+    resid[...] = stream
+    mean = jnp.mean(stream * stream, axis=-1, keepdims=True)
+    normed = (stream * lax.rsqrt(mean + EPSILON) * gain[...]).astype(BF16)
     left_half, right_half = normed[:, :HALF], normed[:, HALF:]
     nsend[...] = jnp.where(c == 0, right_half, left_half)
     nbuf[c] = jnp.where(c == 0, left_half, right_half)
-    lasts = [remote(nsend, nbuf.at[c], e_s.at[0], e_r.at[0], sibling)]
-    lasts[0].start()
 
     row = lax.broadcasted_iota(jnp.int32, (TOK, TOK), 0)
     col = lax.broadcasted_iota(jnp.int32, (TOK, TOK), 1)
@@ -342,100 +418,11 @@
         normed, router[...], (((1,), (1,)), ((), ())), preferred_element_type=F32
     )
     apart = jnp.sum(logits * (hits[0] - hits[1]), axis=-1, keepdims=True)
-    gates = matches[0] * jax.nn.sigmoid(apart) + matches[1] * jax.nn.sigmoid(-apart)
-    coarse = gates.astype(BF16)
-    gbuf[c, 0] = coarse
-    gbuf[c, 1] = (gates - coarse.astype(F32)).astype(BF16)
-    for i, ref in ((1, pbuf), (2, gbuf)):
-        cp = remote(ref.at[c], ref.at[c], e_s.at[i], e_r.at[i], sibling)
-        cp.start()
-        lasts.append(cp)
-    lasts[0].wait_recv()
-    lasts[1].wait_recv()
-    packed_out[...] = (
-        lax.dot_general(
-            pbuf[...].reshape(32, 128), nbuf[...].reshape(32, HALF), (((0,), (0,)), ((), ())),
-            preferred_element_type=F32,
-        )
-        .astype(BF16)
-        .reshape(E, TOK, HALF)
-    )
-    lasts[2].wait_recv()
-    gates_out[...] = gbuf[...]
-
-    for cp in list(firsts.values()) + passes + gathers + lasts:
-        cp.wait_send()
-    for i in range(4):
-        loop(15, lambda k: second(i, k + 1).wait_send())
-    for k in range(8):
-        halves[k].wait_send()
-        for cp in parts[k]:
-            cp.wait_send()
-        if k > 0:
-            ends[k].wait_send()
-
-
-def attention(*operands):
-    dma = pltpu.SemaphoreType.DMA
-    v = pltpu.VMEM
-    return pl.pallas_call(
-        attention_kernel,
-        out_shape=(
-            jax.ShapeDtypeStruct((TOK, D), F32),
-            jax.ShapeDtypeStruct((E, TOK, HALF), BF16),
-            jax.ShapeDtypeStruct((2, 2, TOK, 128), BF16),
-        ),
-        in_specs=[SMEM] + [ANY] * 11 + [VMEM],
-        out_specs=(VMEM,) * 3,
-        scratch_shapes=[v((PASS_DEV, 128, 512), BF16)] * 4
-        + [v((4, N_REQ, 128, 512), BF16)]
-        + [v((16, 128, 256), BF16)] * 4
-        + [
-            v((4, 1024, 256), BF16), v((4, 1024, 256), BF16),
-            v((QTOK, HEADS * HD), BF16), v((QTOK, 256), BF16),
-            v((QTOK, HD), F32), v((QTOK, HD), F32),
-            v((PUSE * GAP, HD), F32), v((PUSE * GAP, HD), F32),
-            v((HEADS * QTOK, HD), BF16),
-            v((HEADS * QTOK, HD), F32), v((HEADS * QTOK, HD), F32), v((HEADS * QTOK, HD), F32),
-            v((8, 2, TOK, 384), BF16), v((384, COLS), BF16), v((TOK, D), BF16), v((1, D), F32),
-            v((E, D), BF16), v((4, 2, 8, 2, TOK, 384), BF16),
-            v((8, 8, TOK, COLS), F32),
-            v((8, 8, TOK, COLS), BF16), v((8, 8, TOK, COLS), BF16),
-            v((8, 8, TOK, COLS), BF16), v((8, 8, TOK, COLS), BF16),
-            v((8, TOK, COLS), BF16), v((8, TOK, COLS), BF16),
-            v((TOK, HALF), BF16), v((2, TOK, HALF), BF16),
-            v((2, TOK, 128), BF16), v((2, 2, TOK, 128), BF16),
-            dma((10,)), dma((4,)), dma((4,)), dma((4, 16)), dma((4, 16)), dma((4,)), dma((4,)),
-            dma((7,)), dma((7,)), dma((8,)), dma((8,)), dma((8, 8)), dma((8, 8)),
-            dma((8,)), dma((8,)), dma((3,)), dma((3,)),
-        ],
-        name="attend_and_project",
-        compiler_params=pltpu.CompilerParams(
-            collective_id=0, has_side_effects=True, vmem_limit_bytes=56 << 20
-        ),
-    )(*operands)
-
-
-def expert_kernel(
-    packed, gates, resid, wg_h, wu_h, wd_h, out,
-    wg, wu, wd, prx, xo, xs, gu, inner, po, sps, spr, rzs, rz, ysend, ry, kept, bsend, ret,
-    mixed, mrecv,
-    w_s, a_s, a_r, y_s, y_r, g_s, g_r, f_s, f_r, p_s, p_r, r_s, r_r, t_s, t_r, m_s, m_r,
-):
-    req, exp, z, yh, c = place()
-    other = 1 - yh
-    sibling = (req, member(z, yh, 1 - c))
-    across = (req, member(z, other, c))
-    up = (req, member((z + 1) % 4, yh, c))
-    down = (req, member((z + 3) % 4, yh, c))
-    peers = [((req + d) % N_REQ, exp) for d in range(1, 8)]
-    loads = [
-        pltpu.make_async_copy(src, dst, w_s.at[i])
-        for i, (src, dst) in enumerate(((wg_h, wg), (wu_h, wu), (wd_h, wd)))
-    ]
-    for cp in loads:
-        cp.start()
-    greet(peers + [sibling, across, up, down])
+    shares_of = matches[0] * jax.nn.sigmoid(apart) + matches[1] * jax.nn.sigmoid(-apart)
+    coarse = shares_of.astype(BF16)
+    gates[c, 0] = coarse
+    gates[c, 1] = (shares_of - coarse.astype(F32)).astype(BF16)
+    pl.semaphore_wait(pltpu.get_barrier_semaphore(), len(friends))
 
     started = []
 
@@ -443,6 +430,22 @@
         cp.start()
         started.append(cp)
         return cp
+
+    lasts = [
+        go(remote(nsend, nbuf.at[c], e_s.at[0], e_r.at[0], sibling)),
+        go(remote(pbuf.at[c], pbuf.at[c], e_s.at[1], e_r.at[1], sibling)),
+        go(remote(gates.at[c], gates.at[c], e_s.at[2], e_r.at[2], sibling)),
+    ]
+    lasts[0].wait_recv()
+    lasts[1].wait_recv()
+    packed[...] = (
+        lax.dot_general(
+            pbuf[...].reshape(32, 128), nbuf[...].reshape(32, HALF), (((0,), (0,)), ((), ())),
+            preferred_element_type=F32,
+        )
+        .astype(BF16)
+        .reshape(E, TOK, HALF)
+    )
 
     def part(i):
         return pl.ds(i * CW, CW)
@@ -692,6 +695,7 @@
     for i in LATE:
         give_back(i)
     mix = {}
+    lasts[2].wait_recv()
     for i in early + list(LATE):
         for cp in back[i]:
             cp.wait_recv()
@@ -716,9 +720,12 @@
     return pl.pallas_call(
         expert_kernel,
         out_shape=jax.ShapeDtypeStruct((TOK, D), BF16),
-        in_specs=[VMEM] * 3 + [ANY] * 3,
+        in_specs=[VMEM] * 2 + [ANY] * 6,
         out_specs=VMEM,
         scratch_shapes=[
+            v((TOK, D), BF16), v((1, D), F32), v((E, D), BF16), v((TOK, D), F32),
+            v((E, TOK, HALF), BF16), v((TOK, HALF), BF16), v((2, TOK, HALF), BF16),
+            v((2, TOK, 128), BF16), v((2, 2, TOK, 128), BF16),
             v((D, HID), BF16), v((D, HID), BF16), v((HID, D), BF16),
             v((NCH, N_REQ, TOK, CW), BF16),
             v((NCH, 4, 2, 80, CW), BF16), v((NCH, 4, 2, 80, CW), BF16),
@@ -729,7 +736,7 @@
             v((NCH, 80, CW), BF16), v((NCH, 80, CW), BF16), v((NCH, 80, CW), F32),
             v((NCH, N_REQ, TOK, CW), BF16), v((NCH, N_REQ, TOK, CW), BF16),
             v((NCH, 2, TOK, CW), F32), v((NCH, TOK, CW), F32),
-            dma((3,)), dma((NCH, 8)), dma((NCH, 8)), dma((NCH,)), dma((NCH,)),
+            dma((6,)), dma((3,)), dma((3,)), dma((NCH, 8)), dma((NCH, 8)), dma((NCH,)), dma((NCH,)),
             dma((8, NCH)), dma((8, NCH)), dma((8, NCH)), dma((8, NCH)),
             dma((NCH, 4)), dma((NCH, 4)), dma((7, NCH)), dma((7, NCH)),
             dma((NCH, 8)), dma((NCH, 8)), dma((NCH,)), dma((NCH,)),
@@ -759,11 +766,13 @@
     qcos, qsin = rotation(PUSE * (PLEN + GAP) + np.arange(QTOK))
     starts = np.arange(PUSE)[:, None] * (PLEN + GAP) + np.arange(GAP)[None, :]
     pcos, psin = rotation(starts.reshape(-1))
-    resid, packed, gates = attention(
-        jnp.concatenate([use_lists, offsets], axis=1), passage_kv, queries, question_kv, qcos, qsin, pcos, psin, out_weight,
-        hidden_in, norm_gain.reshape(1, D), router.T, routes.T,
-    )
-    return experts(packed, gates, resid, w_gate[0], w_up[0], w_down[0])
+    attn = attention(
+        jnp.concatenate([use_lists, offsets], axis=1), passage_kv, queries, question_kv,
+        qcos, qsin, pcos, psin, out_weight,
+    )
+    return experts(
+        attn, routes.T, hidden_in, norm_gain.reshape(1, D), router.T, w_gate[0], w_up[0], w_down[0]
+    )
 
 
 def solution(mesh):

time: 196 us -> 196 us (level)
    pallas_call x1, Pallas kernels: 102 us -> 97.1 us  [attention(): pl.pallas_call(attention_kernel, out_shape=jax.ShapeDtypeStruct((TOK, D),...]
    pallas_call x1, Pallas kernels: 90.3 us -> 94.6 us  [experts(): pl.pallas_call(expert_kernel, out_shape=jax.ShapeDtypeStruct((TOK, D), BF...]
where the time goes in v1:
time: 196 us
  Pallas kernels  192 us (98%)
  local copies, waits for them, and re-layouts  3.13 us (2%)
    pallas_call x1, Pallas kernels, attention(): pl.pallas_call(attention_kernel, out_shape=jax.ShapeDtypeStruct((TOK, D),...  97.1 us
    pallas_call x1, Pallas kernels, experts(): pl.pallas_call(expert_kernel, out_shape=jax.ShapeDtypeStruct((TOK, D), BF...  94.6 us

profile of v1, /device:TPU:1, one launch (start us, length us, event | category | flops | bytes accessed | tf_op | source)
XLA Modules:
  0.0 195.6 jit_solution(8565684618768293902)
XLA Ops:
  0.0 0.8 copy.18
  0.8 0.8 copy.19
  1.5 0.7 pad_add_fusion.table
  2.2 97.1 %attend_and_project.1.attn = bf16[16,6144]{1,0:T(8,128)(2,1)} custom-call(s32[8,8]{1,0:T(8,128)} %pad_add_fusion.table, bf16[4,128,2048]{2,1,0:T(8,128)(2,1)} %pkv.1, bf16[256,384]{1,0:T(8,128)(2,1)} %q_h.1, bf16[256,2048]{1,0:T(8,128)(2,1)} %qkv.1, f32[256,128]{1,0:T(8,128)} %constant.8.clone.qcos_h, f32[256,128]{1,0:T(8,128)} %constant.9.clone.qsin_h, ...), custom_call_target="tpu_custom_call" | custom-call | tf_op jit(solution)/shard_map/attend_and_project/pallas_call | solution.py:334
  99.3 94.6 %apply_experts.1 = bf16[16,6144]{1,0:T(8,128)(2,1)} custom-call(bf16[16,6144]{1,0:T(8,128)(2,1)} %attend_and_project.1.attn, s32[2,16]{1,0:T(2,128)} %bitcast.11, bf16[16,6144]{1,0:T(8,128)(2,1)} %hid_h.1, f32[1,6144]{1,0:T(1,128)} %bitcast.10, bf16[8,6144]{1,0:T(8,128)(2,1)} %bitcast.9, bf16[6144,512]{1,0:T(8,128)(2,1)} %bitcast.6, ...), custom_call_target="tpu_custom_call" | custom-call | tf_op jit(solution)/shard_map/apply_experts/pallas_call | solution.py:720
  193.9 1.6 copy.21

commit v2 on v1

--- a/solution.py
+++ b/solution.py
@@ -158,12 +158,12 @@
     for r in range(N_REQ):
         at = jnp.int32(0)
         for j in range(PUSE):
-            p = table[r, j]
+            p = table[j, r]
             at = at + jnp.where(p // PASS_DEV == req, p % PASS_DEV, 0)
         sel.append(at)
-    own = [table[req, j] // PASS_DEV for j in range(PUSE)]
+    own = [table[j, req] // PASS_DEV for j in range(PUSE)]
     spot = [
-        j * GAP + jnp.clip(table[req, PUSE + j] - j * (PLEN + GAP), 0, GAP - 1) for j in range(PUSE)
+        j * GAP + jnp.clip(table[PUSE + j, req] - j * (PLEN + GAP), 0, GAP - 1) for j in range(PUSE)
     ]
 
     for i, d in enumerate(CHUNKS):
@@ -284,7 +284,7 @@
         return cp
 
     halves, parts, ends, gathers = {}, {}, {}, [swap, right0, left0]
-    for k in range(8 + 4):
+    for k in range(8 + 3):
         if k < 8:
             if k == 1:
                 swap.wait_recv()
@@ -308,8 +308,8 @@
             halves[k] = multiply(k, att if k == 0 else attb.at[order[k][0], order[k][1]])
         if 0 <= k - 1 < 8:
             parts[k - 1] = scatter(k - 1, halves[k - 1])
-        if 0 <= k - 4 < 8:
-            ends[k - 4] = finish(k - 4, parts[k - 4])
+        if 0 <= k - 3 < 8:
+            ends[k - 3] = finish(k - 3, parts[k - 3])
     for k in range(1, 8):
         ends[k].wait_recv()
 
@@ -767,7 +767,7 @@
     starts = np.arange(PUSE)[:, None] * (PLEN + GAP) + np.arange(GAP)[None, :]
     pcos, psin = rotation(starts.reshape(-1))
     attn = attention(
-        jnp.concatenate([use_lists, offsets], axis=1), passage_kv, queries, question_kv,
+        jnp.concatenate([use_lists.T, offsets.T], axis=0), passage_kv, queries, question_kv,
         qcos, qsin, pcos, psin, out_weight,
     )
     return experts(

time: 196 us -> 194 us (0.990)
  no operation moved by 1% of the time
where the time goes in v2:
time: 194 us
  Pallas kernels  191 us (98%)
    pallas_call x1, Pallas kernels, attention(): pl.pallas_call(attention_kernel, out_shape=jax.ShapeDtypeStruct((TOK, D),...  96.6 us
    pallas_call x1, Pallas kernels, experts(): pl.pallas_call(expert_kernel, out_shape=jax.ShapeDtypeStruct((TOK, D), BF...  94.2 us

profile of v2, /device:TPU:1, one launch (start us, length us, event | category | flops | bytes accessed | tf_op | source)
XLA Modules:
  0.0 193.7 jit_solution(3764982030837788172)
XLA Ops:
  0.0 1.3 pad_add_fusion.table
  1.3 96.6 %attend_and_project.1.attn = bf16[16,6144]{1,0:T(8,128)(2,1)} custom-call(s32[8,8]{1,0:T(8,128)} %pad_add_fusion.table, bf16[4,128,2048]{2,1,0:T(8,128)(2,1)} %pkv.1, bf16[256,384]{1,0:T(8,128)(2,1)} %q_h.1, bf16[256,2048]{1,0:T(8,128)(2,1)} %qkv.1, f32[256,128]{1,0:T(8,128)} %constant.8.clone.qcos_h, f32[256,128]{1,0:T(8,128)} %constant.9.clone.qsin_h, ...), custom_call_target="tpu_custom_call" | custom-call | tf_op jit(solution)/shard_map/attend_and_project/pallas_call | solution.py:334
  97.9 94.2 %apply_experts.1 = bf16[16,6144]{1,0:T(8,128)(2,1)} custom-call(bf16[16,6144]{1,0:T(8,128)(2,1)} %attend_and_project.1.attn, s32[2,16]{1,0:T(2,128)} %bitcast.15, bf16[16,6144]{1,0:T(8,128)(2,1)} %hid_h.1, f32[1,6144]{1,0:T(1,128)} %bitcast.12, bf16[8,6144]{1,0:T(8,128)(2,1)} %bitcast.11, bf16[6144,512]{1,0:T(8,128)(2,1)} %bitcast.8, ...), custom_call_target="tpu_custom_call" | custom-call | tf_op jit(solution)/shard_map/apply_experts/pallas_call | solution.py:720
  192.1 1.6 copy.19
